TPU v7x, 32 devices: a whole 2x2x4 slice. The times are simulated.
32 devices in a mesh: grp: 4 (over z), narrow: 8 (over y, x, core).
Axes of the slice: x: 2, y: 2, z: 4, core: 2. Of those that a mesh axis runs over, the one named last changes fastest.
Arguments:
- panel: bfloat16 [64, 57344], P(None, ('grp', 'narrow')), may hold values from -6 to 6
- tiles: bfloat16 [16384, 128, 128], P(('grp', 'narrow')), may hold values from -0.125 to 0.125
- tile_row: int32 [16384], P(('grp', 'narrow')), may hold values from 0 to 447, as said below
- tile_col: int32 [16384], P(('grp', 'narrow')), may hold values from 0 to 447, as said below
- tile_count: int32 [32], P(('grp', 'narrow')), may hold values from 128 to 512, as said below
Outputs:
- filtered: bfloat16 [64, 57344], P(None, ('grp', 'narrow'))
- normal_image: float32 [64, 57344], P(None, ('grp', 'narrow'))
Inputs may be any that keep to these rules, and one draw needn't show every extreme that they name: tile_row of a slot on a device of grp index g lies in g * 112 .. (g + 1) * 112 - 1. tile_col of a slot on a device of grp index g lies in (g - 1) * 112 .. (g + 1) * 112 - 1, and in g * 112 .. for g = 0. `tile_count`: some device holds 512 live slots.
All inputs are finite; a program needn't handle non-finite values.
Results may differ from a plain program's by a relative error of at most 0.009.
Values may be sent and summed in bfloat16 or wider, within the bound.
A program may use at most 128 MiB of HBM per device.

v0:
```python
import functools

import jax
import jax.numpy as jnp
from jax import lax
from jax.experimental import pallas as pl
from jax.experimental.pallas import tpu as pltpu
from jax.sharding import PartitionSpec as P

MESH = pl.DeviceIdType.MESH
VMEM_LIMIT = 56 * 1024 * 1024
BATCH = 32
DELAY = 4
CHUNKS = 4
PLAIN, ALONG = (0, 1), (2, 3)
ANY = pl.BlockSpec(memory_space=pl.ANY)
VMEM = pl.BlockSpec(memory_space=pltpu.VMEM)


def flip(index, mask):
    bit = 1
    while bit <= mask:
        if mask & bit:
            index = index + bit - 2 * bit * ((index // bit) % 2)
        bit *= 2
    return index


def bits_of(n):
    bits = []
    while 2 ** len(bits) < n:
        bits.append(2 ** len(bits))
    return bits


def spread_orders(n):
    bits = bits_of(n)
    return [bits[1:] + bits[:1], bits[:0:-1] + bits[:1]] * (CHUNKS // 2)


def sum_orders(n):
    bits = bits_of(n)
    return [bits[:1] + bits[1:], bits[:1] + bits[:0:-1]] * (CHUNKS // 2)


def chunks_of(nbd):
    big = -(-nbd // CHUNKS)
    edges = [0, big, 2 * big, 2 * big + (nbd - 2 * big) // 2, nbd]
    return [(low, high - low) for low, high in zip(edges, edges[1:])]


def greet(n, group, groups, me, along_grp):
    barrier = pltpu.get_barrier_semaphore()
    bits = bits_of(n)
    for bit in bits:
        pl.semaphore_signal(barrier, inc=1, device_id=(group, flip(me, bit)), device_id_type=MESH)
    if along_grp:
        @pl.when(group > 0)
        def _():
            pl.semaphore_signal(barrier, inc=1, device_id=(group - 1, me), device_id_type=MESH)

        @pl.when(group < groups - 1)
        def _():
            pl.semaphore_signal(barrier, inc=1, device_id=(group + 1, me), device_id_type=MESH)

        ends = jnp.minimum(group, 1) + jnp.minimum(groups - 1 - group, 1)
        pl.semaphore_wait(barrier, len(bits) + ends)
    else:
        pl.semaphore_wait(barrier, len(bits))


def spread_steps(n):
    steps = []
    for chunk, order in enumerate(spread_orders(n)):
        place = {bit: k for k, bit in enumerate(order)}
        for r in range(n):
            held = [place[bit] for bit in order if r & bit]
            last = max(held) if held else -1
            steps.append((len(held), chunk, r, order[last + 1:]))
    return [step[1:] for step in sorted(steps, key=lambda s: (s[0], s[2], s[1]))]


def spread_copy(n, nbd, group, me, own, out, base, send, recv, chunk, r, bit):
    start, size = chunks_of(nbd)[chunk]
    at = pl.ds(base + flip(me, r) * nbd + start, size)
    source = out.at[at] if r or own is None else own.at[pl.ds(start, size)]
    return pltpu.make_async_remote_copy(
        src_ref=source, dst_ref=out.at[at],
        send_sem=send.at[chunk, r | bit], recv_sem=recv.at[chunk, r | bit],
        device_id=(group, flip(me, bit)), device_id_type=MESH)


def spread_here(args, chunk, r):
    if r:
        last = [bit for bit in spread_orders(args[0])[chunk] if r & bit][-1]
        spread_copy(*args, chunk, r - last, last).wait_recv()


def spread_own(args, chunks):
    orders = spread_orders(args[0])
    for k in range(len(orders[0])):
        for chunk in chunks:
            spread_copy(*args, chunk, 0, orders[chunk][k]).start()


def spread_level(args, level, chunks, also=None):
    for chunk, r, sends in spread_steps(args[0]):
        if chunk in chunks and bin(r).count("1") == level and sends:
            spread_here(args, chunk, r)
            for bit in sends:
                spread_copy(*args, chunk, r, bit).start()
            if also is not None:
                also(chunk, r)


def spread_ends(args, chunks):
    for chunk, r, sends in spread_steps(args[0]):
        if chunk in chunks and r and not sends:
            spread_here(args, chunk, r)


def spread_finish(n, nbd, group, me, own, out, base, send, recv, chunks):
    copy = functools.partial(spread_copy, n, nbd, group, me, own, out, base, send, recv)
    for chunk, r, sends in spread_steps(n):
        for bit in sends if chunk in chunks else ():
            copy(chunk, r, bit).wait_send()


def gather_kernel(n, groups, panel, out, mine, send, recv, psend, precv, zsend, zrecv, lsem):
    group, me = lax.axis_index("grp"), lax.axis_index("narrow")
    nbd = mine.shape[0]
    nbg = n * nbd
    levels = len(bits_of(n))
    every = range(CHUNKS)
    evens = sorted(range(0, n, 2), key=lambda r: bin(r).count("1"))
    for j in range(nbd):
        mine[j] = panel[:, j * 128:(j + 1) * 128]
    greet(n, group, groups, me, True)

    def zcopy(chunk, r, target):
        start, size = chunks_of(nbd)[chunk]
        at = flip(me, r) * nbd + start
        source = out.at[pl.ds(nbg + at, size)] if r else mine.at[pl.ds(start, size)]
        return pltpu.make_async_remote_copy(
            src_ref=source, dst_ref=out.at[pl.ds(at, size)],
            send_sem=zsend.at[chunk, r], recv_sem=zrecv.at[chunk, r],
            device_id=(target, me), device_id_type=MESH)

    own = (n, nbd, group, me, mine, out, nbg, send, recv)
    prior = (n, nbd, group, me, None, out, 0, psend, precv)

    @pl.when(group < groups - 1)
    def _():
        for chunk in every:
            zcopy(chunk, 0, group + 1).start()

    spread_own(own, every)
    keep = pltpu.make_async_copy(mine, out.at[pl.ds(nbg + me * nbd, nbd)], lsem.at[0])
    keep.start()

    def up(chunk, r):
        if chunk in ALONG and r % 2 == 0:
            @pl.when(group < groups - 1)
            def _():
                zcopy(chunk, r, group + 1).start()

    for level in range(1, levels):
        spread_level(own, level, every, up)

        @pl.when(group > 0)
        def _():
            if level == 1:
                for chunk in PLAIN:
                    zcopy(chunk, 0, group - 1).wait_recv()
                spread_own(prior, PLAIN)
            for r in evens:
                if bin(r).count("1") == level - 1:
                    for chunk in ALONG:
                        zcopy(chunk, r, group - 1).wait_recv()
                        spread_copy(*prior, chunk, r, 1).start()

    @pl.when(group > 0)
    def _():
        for level in range(1, levels):
            spread_level(prior, level, PLAIN)
        for r in evens:
            if bin(r).count("1") >= levels - 1:
                for chunk in ALONG:
                    zcopy(chunk, r, group - 1).wait_recv()
                    spread_copy(*prior, chunk, r, 1).start()

    spread_ends(own, every)

    @pl.when(group > 0)
    def _():
        spread_ends(prior, PLAIN)
        spread_finish(*prior, PLAIN)
        for chunk in ALONG:
            for r in evens:
                spread_copy(*prior, chunk, r, 1).wait()

    spread_finish(*own, every)
    keep.wait()

    @pl.when(group < groups - 1)
    def _():
        for chunk in every:
            for r in evens if chunk in ALONG else (0,):
                zcopy(chunk, r, group + 1).wait_send()


def gather(n, groups, nbd, panel):
    cols = panel.shape[0]
    nbg = n * nbd
    return pl.pallas_call(
        functools.partial(gather_kernel, n, groups),
        out_shape=jax.ShapeDtypeStruct((2 * nbg, cols, 128), jnp.bfloat16),
        in_specs=[VMEM],
        out_specs=ANY,
        scratch_shapes=[
            pltpu.VMEM((nbd, cols, 128), jnp.bfloat16),
            pltpu.SemaphoreType.DMA((CHUNKS, n)),
            pltpu.SemaphoreType.DMA((CHUNKS, n)),
            pltpu.SemaphoreType.DMA((CHUNKS, n)),
            pltpu.SemaphoreType.DMA((CHUNKS, n)),
            pltpu.SemaphoreType.DMA((CHUNKS, n)),
            pltpu.SemaphoreType.DMA((CHUNKS, n)),
            pltpu.SemaphoreType.DMA((1,)),
        ],
        compiler_params=pltpu.CompilerParams(
            collective_id=1, has_side_effects=True, vmem_limit_bytes=VMEM_LIMIT),
        name="gather_panel",
    )(panel)


def apply_kernel(forward, block, nbg, rows, cols, count, src, tiles, *rest):
    if forward:
        out, acc = rest
    else:
        out, filtered, acc = rest
    step = pl.program_id(0)
    live = count[0]
    group = lax.axis_index("grp")
    row0, col0 = group * nbg, (group - 1) * nbg
    nout = out.shape[0]

    @pl.when(step == 0)
    def _():
        acc[...] = jnp.zeros_like(acc)
        if not forward:
            nbd = filtered.shape[1] // 128
            first_own = lax.axis_index("narrow") * nbd
            for j in range(nbd):
                filtered[:, j * 128:(j + 1) * 128] = src[first_own + j]

    first = step * block
    here = jnp.clip(live - first, 0, block)

    def batch(b, carry):
        waiting = []

        def add():
            place, prod = waiting.pop(0)
            acc[place] += prod

        for u in range(BATCH):
            at = b * BATCH + u
            slot = first + at
            row, col = rows[slot] - row0, cols[slot] - col0
            source, place = (col, row) if forward else (row, col)
            prod = lax.dot_general(
                src[source], tiles[at], (((1,), (1 if forward else 0,)), ((), ())),
                preferred_element_type=jnp.float32)
            waiting.append((jnp.where(slot < live, place, nout), prod))
            if len(waiting) > DELAY:
                add()
        while waiting:
            add()
        return carry

    lax.fori_loop(0, (here + BATCH - 1) // BATCH, batch, 0)

    @pl.when(step == pl.num_programs(0) - 1)
    def _():
        def put(j, carry):
            out[j] = acc[j].astype(out.dtype)
            return carry
        lax.fori_loop(0, nout, put, 0, unroll=8)


def apply_tiles(forward, nbg, nbd, src, tiles, tile_row, tile_col, tile_count):
    slots, tile = tiles.shape[:2]
    kcols = src.shape[1]
    block = min(64, slots)
    nin, nout = (2 * nbg, nbg) if forward else (nbg, 2 * nbg)
    whole = lambda i, r, c, n: (0, 0, 0)
    sums = jax.ShapeDtypeStruct((nout, kcols, tile), jnp.bfloat16)
    sums_spec = pl.BlockSpec((nout, kcols, tile), whole)
    own = jax.ShapeDtypeStruct((kcols, nbd * tile), jnp.bfloat16)
    own_spec = pl.BlockSpec((kcols, nbd * tile), lambda i, r, c, n: (0, 0))
    return pl.pallas_call(
        functools.partial(apply_kernel, forward, block, nbg),
        out_shape=sums if forward else (sums, own),
        grid_spec=pltpu.PrefetchScalarGridSpec(
            num_scalar_prefetch=3,
            grid=(slots // block,),
            in_specs=[
                pl.BlockSpec((nin, kcols, tile), whole),
                pl.BlockSpec(
                    (block, tile, tile),
                    lambda i, r, c, n: (jnp.minimum(i, jnp.maximum(n[0] - 1, 0) // block), 0, 0)),
            ],
            out_specs=sums_spec if forward else (sums_spec, own_spec),
            scratch_shapes=[pltpu.VMEM((nout + 1, kcols, tile), jnp.float32)],
        ),
        compiler_params=pltpu.CompilerParams(
            dimension_semantics=("arbitrary",), vmem_limit_bytes=VMEM_LIMIT),
        name="apply_forward" if forward else "apply_transposed",
    )(tile_row, tile_col, tile_count, src, tiles)


class Summed:
    def __init__(self, n, nbd, group, me, part, base, local, lsem, staged, landed, send, recv):
        self.n, self.nbd, self.group, self.me = n, nbd, group, me
        self.part, self.base, self.local, self.lsem = part, base, local, lsem
        self.staged, self.landed, self.send, self.recv = staged, landed, send, recv
        self.orders = sum_orders(n)

    def fetch(self, r):
        at = pl.ds(self.base + flip(self.me, r) * self.nbd, self.nbd)
        return pltpu.make_async_copy(self.part.at[at], self.local.at[r // 2], self.lsem.at[r // 2])

    def begin(self):
        for r in range(0, self.n, 2):
            self.fetch(r).start()

    def fetched(self):
        for r in range(0, self.n, 2):
            self.fetch(r).wait()

    def copy(self, chunk, r):
        order = self.orders[chunk]
        bit = [b for b in order if r & b][0]
        start, size = chunks_of(self.nbd)[chunk]
        if bit == order[0]:
            source = self.part.at[pl.ds(self.base + flip(self.me, r) * self.nbd + start, size)]
        else:
            source = self.staged.at[r, pl.ds(start, size)]
        return pltpu.make_async_remote_copy(
            src_ref=source, dst_ref=self.landed.at[r, pl.ds(start, size)],
            send_sem=self.send.at[chunk, r], recv_sem=self.recv.at[chunk, r],
            device_id=(self.group, flip(self.me, bit)), device_id_type=MESH)

    def sent_at(self, chunk, stage):
        order = self.orders[chunk]
        done = sum(order[:stage])
        rest = [r for r in range(self.n) if r & order[stage] and not r & done]

        def needed(r):
            later = [k for k, b in enumerate(order) if r & b and k > stage]
            return later[0] if later else len(order)

        return sorted(rest, key=needed)

    def value(self, chunk, r, stage, put, more=None):
        order = self.orders[chunk]
        start, size = chunks_of(self.nbd)[chunk]
        for bit in order[:stage]:
            self.copy(chunk, r | bit).wait_recv()
        for j in range(start, start + size):
            total = self.local[r // 2, j].astype(jnp.float32)
            for bit in order[:stage]:
                total = total + self.landed[r | bit, j].astype(jnp.float32)
            if more is not None:
                total = total + more[r // 2, j].astype(jnp.float32)
            put(j, total)

    def stage(self, stage, chunks, ready=None, more=None):
        for chunk in chunks:
            for r in self.sent_at(chunk, stage):
                if stage:
                    def put(j, total, r=r):
                        self.staged[r, j] = total.astype(jnp.bfloat16)
                    if ready is not None:
                        ready(chunk, r)
                    self.value(chunk, r, stage, put, more)
                self.copy(chunk, r).start()

    def finish(self, chunk, put, more=None):
        self.value(chunk, 0, len(self.orders[chunk]), put, more)

    def drain(self, first_stage_only=()):
        for chunk in range(CHUNKS):
            for r in range(1, self.n):
                if chunk not in first_stage_only or r & self.orders[chunk][0]:
                    self.copy(chunk, r).wait_send()


def reduce_kernel(n, groups, part, out, mine, local, psem, staged, landed, send, recv, gsend, grecv, lsem):
    group, me = lax.axis_index("grp"), lax.axis_index("narrow")
    nbd = mine.shape[0]
    greet(n, group, groups, me, False)
    summed = Summed(n, nbd, group, me, part, 0, local, psem, staged, landed, send, recv)
    every = range(CHUNKS)
    summed.stage(0, every)
    summed.begin()
    summed.fetched()
    for stage in range(1, len(bits_of(n))):
        summed.stage(stage, every)

    def put(j, total):
        mine[j] = total.astype(jnp.bfloat16)

    args = (n, nbd, group, me, mine, out, 0, gsend, grecv)
    for pair in range(0, CHUNKS, 2):
        for chunk in (pair, pair + 1):
            summed.finish(chunk, put)
        spread_own(args, (pair, pair + 1))
    keep = pltpu.make_async_copy(mine, out.at[pl.ds(me * nbd, nbd)], lsem.at[0])
    keep.start()
    for level in range(1, len(bits_of(n))):
        spread_level(args, level, every)
    spread_ends(args, every)
    summed.drain()
    spread_finish(*args, every)
    keep.wait()


def reduce_rows(n, groups, nbd, part):
    nbg, cols = part.shape[:2]
    return pl.pallas_call(
        functools.partial(reduce_kernel, n, groups),
        out_shape=jax.ShapeDtypeStruct((nbg, cols, 128), jnp.bfloat16),
        in_specs=[ANY],
        out_specs=ANY,
        scratch_shapes=[
            pltpu.VMEM((nbd, cols, 128), jnp.bfloat16),
            pltpu.VMEM((n // 2, nbd, cols, 128), jnp.bfloat16),
            pltpu.SemaphoreType.DMA((n // 2,)),
            pltpu.VMEM((n, nbd, cols, 128), jnp.bfloat16),
            pltpu.VMEM((n, nbd, cols, 128), jnp.bfloat16),
            pltpu.SemaphoreType.DMA((CHUNKS, n)),
            pltpu.SemaphoreType.DMA((CHUNKS, n)),
            pltpu.SemaphoreType.DMA((CHUNKS, n)),
            pltpu.SemaphoreType.DMA((CHUNKS, n)),
            pltpu.SemaphoreType.DMA((1,)),
        ],
        compiler_params=pltpu.CompilerParams(
            collective_id=2, has_side_effects=True, vmem_limit_bytes=VMEM_LIMIT),
        name="reduce_rows",
    )(part)


def image_kernel(n, groups, part, out, plocal, olocal, pfetch, ofetch, pstaged, planded, ostaged, olanded,
                 psend, precv, osend, orecv, zstaged, zlanded, zsend, zrecv):
    group, me = lax.axis_index("grp"), lax.axis_index("narrow")
    nbd = zstaged.shape[1]
    stages = len(bits_of(n))
    greet(n, group, groups, me, True)
    prior = Summed(n, nbd, group, me, part, 0, plocal, pfetch, pstaged, planded, psend, precv)
    own = Summed(n, nbd, group, me, part, n * nbd, olocal, ofetch, ostaged, olanded, osend, orecv)

    def zcopy(chunk, r, target):
        at = pl.ds(*chunks_of(nbd)[chunk])
        return pltpu.make_async_remote_copy(
            src_ref=zstaged.at[r // 2, at], dst_ref=zlanded.at[r // 2, at],
            send_sem=zsend.at[chunk, r], recv_sem=zrecv.at[chunk, r],
            device_id=(target, me), device_id_type=MESH)

    def down(chunk, r, stage):
        def put(j, total):
            zstaged[r // 2, j] = total.astype(jnp.bfloat16)
        prior.value(chunk, r, stage, put)
        zcopy(chunk, r, group - 1).start()

    def ready(chunk, r):
        @pl.when(group < groups - 1)
        def _():
            zcopy(chunk, r, group + 1).wait_recv()

    @pl.when(group > 0)
    def _():
        prior.stage(0, ALONG + PLAIN)
        prior.begin()

    own.stage(0, PLAIN + ALONG)
    own.begin()

    @pl.when(group == groups - 1)
    def _():
        zlanded[...] = jnp.zeros_like(zlanded)

    @pl.when(group > 0)
    def _():
        prior.fetched()
        for r in sorted(range(0, n, 2), reverse=True):
            for chunk in ALONG:
                down(chunk, r, 1)
        prior.stage(1, PLAIN)

    own.fetched()
    own.stage(1, PLAIN)
    for stage in range(2, stages):
        @pl.when(group > 0)
        def _():
            prior.stage(stage, PLAIN)
    own.stage(1, ALONG, ready, zlanded)

    @pl.when(group > 0)
    def _():
        for chunk in PLAIN:
            down(chunk, 0, stages)

    for stage in range(2, stages):
        own.stage(stage, PLAIN)
        own.stage(stage, ALONG, ready, zlanded)

    def put_own(j, total):
        out[:, j * 128:(j + 1) * 128] = total

    for chunk in ALONG + PLAIN:
        ready(chunk, 0)
        own.finish(chunk, put_own, zlanded)

    own.drain()

    @pl.when(group > 0)
    def _():
        prior.drain(ALONG)
        for chunk in range(CHUNKS):
            for r in range(0, n, 2) if chunk in ALONG else (0,):
                zcopy(chunk, r, group - 1).wait_send()


def image(n, groups, nbd, part):
    cols = part.shape[1]
    held = pltpu.VMEM((n, nbd, cols, 128), jnp.bfloat16)
    evens = pltpu.VMEM((n // 2, nbd, cols, 128), jnp.bfloat16)
    fetch = pltpu.SemaphoreType.DMA((n // 2,))
    sems = pltpu.SemaphoreType.DMA((CHUNKS, n))
    return pl.pallas_call(
        functools.partial(image_kernel, n, groups),
        out_shape=jax.ShapeDtypeStruct((cols, nbd * 128), jnp.float32),
        in_specs=[ANY],
        out_specs=VMEM,
        scratch_shapes=[evens, evens, fetch, fetch, held, held, held, held, sems, sems, sems, sems,
                        evens, evens, sems, sems],
        compiler_params=pltpu.CompilerParams(
            collective_id=3, has_side_effects=True, vmem_limit_bytes=VMEM_LIMIT),
        name="image_sums",
    )(part)


def body(panel, tiles, tile_row, tile_col, tile_count):
    tile = tiles.shape[1]
    nbd = panel.shape[1] // tile
    n, groups = lax.axis_size("narrow"), lax.axis_size("grp")
    nbg = nbd * n
    both = gather(n, groups, nbd, panel)
    part = apply_tiles(True, nbg, nbd, both, tiles, tile_row, tile_col, tile_count)
    rows = reduce_rows(n, groups, nbd, part)
    sums, filtered = apply_tiles(False, nbg, nbd, rows, tiles, tile_row, tile_col, tile_count)
    return filtered, image(n, groups, nbd, sums)


def solution(mesh):
    spread = P(("grp", "narrow"))
    columns = P(None, ("grp", "narrow"))
    return jax.shard_map(
        body,
        mesh=mesh,
        in_specs=(columns, P(("grp", "narrow"), None, None), spread, spread, spread),
        out_specs=(columns, columns),
        check_vma=False,
    )
```

profile of v0, /device:TPU:0, one launch (start us, length us, event | category | flops | bytes accessed | tf_op | source)
XLA Modules:
  0.0 106.0 jit_solution(6077617996927737743)
XLA Ops:
  1.3 19.8 %gather_panel.1.src = bf16[224,64,128]{2,1,0:T(8,128)(2,1)} custom-call(bf16[64,1792]{1,0:T(8,128)(2,1)} %panel.1), custom_call_target="tpu_custom_call" | custom-call | tf_op jit(solution)/shard_map/gather_panel/pallas_call | solution.py:215
  21.1 18.7 %apply_forward.1.part = bf16[112,64,128]{2,1,0:T(8,128)(2,1)} custom-call(s32[512]{0:T(512)} %rows.3, s32[512]{0:T(512)} %cols.3, s32[1]{0:T(128)S(6)} %copy.8.count, bf16[224,64,128]{2,1,0:T(8,128)(2,1)} %gather_panel.1.src, bf16[512,128,128]{2,1,0:T(8,128)(2,1)} %tiles.3), custom_call_target="tpu_custom_call" | custom-call | tf_op jit(solution)/shard_map/apply_forward/pallas_call | solution.py:301
  39.8 24.6 %reduce_rows.1.src = bf16[112,64,128]{2,1,0:T(8,128)(2,1)} custom-call(bf16[112,64,128]{2,1,0:T(8,128)(2,1)} %apply_forward.1.part), custom_call_target="tpu_custom_call" | custom-call | tf_op jit(solution)/shard_map/reduce_rows/pallas_call | solution.py:431
  64.4 15.2 %apply_transposed.1 = (bf16[224,64,128]{2,1,0:T(8,128)(2,1)}, bf16[64,1792]{1,0:T(8,128)(2,1)}) custom-call(s32[512]{0:T(512)} %rows.3, s32[512]{0:T(512)} %cols.3, s32[1]{0:T(128)S(6)} %copy.8.count, bf16[112,64,128]{2,1,0:T(8,128)(2,1)} %reduce_rows.1.src, bf16[512,128,128]{2,1,0:T(8,128)(2,1)} %tiles.3), custom_call_target="tpu_custom_call" | custom-call | tf_op jit(solution)/shard_map/apply_transposed/pallas_call | solution.py:301
  79.6 24.5 %image_sums.1 = f32[64,1792]{1,0:T(8,128)} custom-call(bf16[224,64,128]{2,1,0:T(8,128)(2,1)} %get-tuple-element.5.part), custom_call_target="tpu_custom_call" | custom-call | tf_op jit(solution)/shard_map/image_sums/pallas_call | solution.py:541
  104.2 1.8 %copy.9 = f32[64,1792]{1,0:T(8,128)} copy(f32[64,1792]{1,0:T(8,128)} %image_sums.1) | data formatting | bytes 917504
where the time goes:
time: 106 us
  Pallas kernels  103 us (97%)
  local copies, waits for them, and re-layouts  1.82 us (2%)
  between operations  1.3 us (1%)
    pallas_call x2, Pallas kernels, apply_tiles(): pl.pallas_call(functools.partial(apply_kernel, forward, block, nbg), out_...  33.9 us
    pallas_call x1, Pallas kernels, reduce_rows(): pl.pallas_call(functools.partial(reduce_kernel, n, groups), out_shape=jax...  24.6 us
    pallas_call x1, Pallas kernels, image(): pl.pallas_call(functools.partial(image_kernel, n, groups), out_shape=jax....  24.5 us
    pallas_call x1, Pallas kernels, gather(): pl.pallas_call(functools.partial(gather_kernel, n, groups), out_shape=jax...  19.8 us

commit v1 on v0

--- a/solution.py
+++ b/solution.py
@@ -216,7 +216,7 @@
         functools.partial(gather_kernel, n, groups),
         out_shape=jax.ShapeDtypeStruct((2 * nbg, cols, 128), jnp.bfloat16),
         in_specs=[VMEM],
-        out_specs=ANY,
+        out_specs=VMEM,
         scratch_shapes=[
             pltpu.VMEM((nbd, cols, 128), jnp.bfloat16),
             pltpu.SemaphoreType.DMA((CHUNKS, n)),
@@ -233,11 +233,11 @@
     )(panel)
 
 
-def apply_kernel(forward, block, nbg, rows, cols, count, src, tiles, *rest):
+def apply_kernel(forward, block, nbg, rows, cols, count, source_blocks, tiles, *rest):
     if forward:
-        out, acc = rest
+        sums, acc, src, out, fetched, sent = rest
     else:
-        out, filtered, acc = rest
+        sums, filtered, acc, src, out, fetched, sent = rest
     step = pl.program_id(0)
     live = count[0]
     group = lax.axis_index("grp")
@@ -246,7 +246,10 @@
 
     @pl.when(step == 0)
     def _():
+        fetch = pltpu.make_async_copy(source_blocks, src, fetched.at[0])
+        fetch.start()
         acc[...] = jnp.zeros_like(acc)
+        fetch.wait()
         if not forward:
             nbd = filtered.shape[1] // 128
             first_own = lax.axis_index("narrow") * nbd
@@ -282,10 +285,18 @@
 
     @pl.when(step == pl.num_programs(0) - 1)
     def _():
-        def put(j, carry):
-            out[j] = acc[j].astype(out.dtype)
-            return carry
-        lax.fori_loop(0, nout, put, 0, unroll=8)
+        parts = sent.shape[0]
+        size = nout // parts
+        for k in range(parts):
+            def put(j, carry):
+                out[j] = acc[j].astype(out.dtype)
+                return carry
+            lax.fori_loop(k * size, (k + 1) * size, put, 0, unroll=4)
+            at = pl.ds(k * size, size)
+            pltpu.make_async_copy(out.at[at], sums.at[at], sent.at[k]).start()
+        for k in range(parts):
+            at = pl.ds(k * size, size)
+            pltpu.make_async_copy(out.at[at], sums.at[at], sent.at[k]).wait()
 
 
 def apply_tiles(forward, nbg, nbd, src, tiles, tile_row, tile_col, tile_count):
@@ -293,9 +304,7 @@
     kcols = src.shape[1]
     block = min(64, slots)
     nin, nout = (2 * nbg, nbg) if forward else (nbg, 2 * nbg)
-    whole = lambda i, r, c, n: (0, 0, 0)
     sums = jax.ShapeDtypeStruct((nout, kcols, tile), jnp.bfloat16)
-    sums_spec = pl.BlockSpec((nout, kcols, tile), whole)
     own = jax.ShapeDtypeStruct((kcols, nbd * tile), jnp.bfloat16)
     own_spec = pl.BlockSpec((kcols, nbd * tile), lambda i, r, c, n: (0, 0))
     return pl.pallas_call(
@@ -305,13 +314,19 @@
             num_scalar_prefetch=3,
             grid=(slots // block,),
             in_specs=[
-                pl.BlockSpec((nin, kcols, tile), whole),
+                ANY,
                 pl.BlockSpec(
                     (block, tile, tile),
                     lambda i, r, c, n: (jnp.minimum(i, jnp.maximum(n[0] - 1, 0) // block), 0, 0)),
             ],
-            out_specs=sums_spec if forward else (sums_spec, own_spec),
-            scratch_shapes=[pltpu.VMEM((nout + 1, kcols, tile), jnp.float32)],
+            out_specs=ANY if forward else (ANY, own_spec),
+            scratch_shapes=[
+                pltpu.VMEM((nout + 1, kcols, tile), jnp.float32),
+                pltpu.VMEM((nin, kcols, tile), jnp.bfloat16),
+                pltpu.VMEM((nout, kcols, tile), jnp.bfloat16),
+                pltpu.SemaphoreType.DMA((1,)),
+                pltpu.SemaphoreType.DMA((4,)),
+            ],
         ),
         compiler_params=pltpu.CompilerParams(
             dimension_semantics=("arbitrary",), vmem_limit_bytes=VMEM_LIMIT),
@@ -432,7 +447,7 @@
         functools.partial(reduce_kernel, n, groups),
         out_shape=jax.ShapeDtypeStruct((nbg, cols, 128), jnp.bfloat16),
         in_specs=[ANY],
-        out_specs=ANY,
+        out_specs=VMEM,
         scratch_shapes=[
             pltpu.VMEM((nbd, cols, 128), jnp.bfloat16),
             pltpu.VMEM((n // 2, nbd, cols, 128), jnp.bfloat16),
@@ -551,6 +566,21 @@
     )(part)
 
 
+def leave_kernel(sums, out):
+    out[...] = sums[...]
+
+
+def leave(sums):
+    return pl.pallas_call(
+        leave_kernel,
+        out_shape=jax.ShapeDtypeStruct(sums.shape, sums.dtype),
+        in_specs=[VMEM],
+        out_specs=VMEM,
+        compiler_params=pltpu.CompilerParams(vmem_limit_bytes=VMEM_LIMIT),
+        name="leave",
+    )(sums)
+
+
 def body(panel, tiles, tile_row, tile_col, tile_count):
     tile = tiles.shape[1]
     nbd = panel.shape[1] // tile
@@ -560,7 +590,7 @@
     part = apply_tiles(True, nbg, nbd, both, tiles, tile_row, tile_col, tile_count)
     rows = reduce_rows(n, groups, nbd, part)
     sums, filtered = apply_tiles(False, nbg, nbd, rows, tiles, tile_row, tile_col, tile_count)
-    return filtered, image(n, groups, nbd, sums)
+    return filtered, leave(image(n, groups, nbd, sums))
 
 
 def solution(mesh):

time: 106 us -> 111 us (1.047)
  Pallas kernels: 103 us -> 109 us
  local copies, waits for them, and re-layouts: 1.82 us -> 0 us
    pallas_call x2, Pallas kernels: 33.9 us -> 24.1 us  [apply_tiles(): pl.pallas_call(functools.partial(apply_kernel, forward, block, nbg), out_...]
    pallas_call x1, Pallas kernels: 24.5 us -> 31.9 us  [image(): pl.pallas_call(functools.partial(image_kernel, n, groups), out_shape=jax....]
    pallas_call x1, Pallas kernels: 24.6 us -> 30.5 us  [reduce_rows(): pl.pallas_call(functools.partial(reduce_kernel, n, groups), out_shape=jax...]
    unnamed x1 -> x0, local copies, waits for them, and re-layouts: 1.82 us -> none
    pallas_call x0 -> x1, Pallas kernels: none -> 1.82 us  [leave(): pl.pallas_call(leave_kernel, out_shape=jax.ShapeDtypeStruct(sums.shape, s...]
where the time goes in v1:
time: 111 us
  Pallas kernels  109 us (98%)
  between operations  1.32 us (1%)
    pallas_call x1, Pallas kernels, image(): pl.pallas_call(functools.partial(image_kernel, n, groups), out_shape=jax....  31.9 us
    pallas_call x1, Pallas kernels, reduce_rows(): pl.pallas_call(functools.partial(reduce_kernel, n, groups), out_shape=jax...  30.5 us
    pallas_call x2, Pallas kernels, apply_tiles(): pl.pallas_call(functools.partial(apply_kernel, forward, block, nbg), out_...  24.1 us
    pallas_call x1, Pallas kernels, gather(): pl.pallas_call(functools.partial(gather_kernel, n, groups), out_shape=jax...  20.9 us

profile of v1, /device:TPU:0, one launch (start us, length us, event | category | flops | bytes accessed | tf_op | source)
XLA Modules:
  0.0 110.5 jit_solution(7821422623913478735)
XLA Ops:
  1.3 20.9 %gather_panel.1.source_blocks = bf16[224,64,128]{2,1,0:T(8,128)(2,1)} custom-call(bf16[64,1792]{1,0:T(8,128)(2,1)} %panel.1), custom_call_target="tpu_custom_call" | custom-call | tf_op jit(solution)/shard_map/gather_panel/pallas_call | solution.py:215
  22.2 12.8 %apply_forward.1.part = bf16[112,64,128]{2,1,0:T(8,128)(2,1)} custom-call(s32[512]{0:T(512)} %rows.3, s32[512]{0:T(512)} %cols.3, s32[1]{0:T(128)S(6)} %copy.7.count, bf16[224,64,128]{2,1,0:T(8,128)(2,1)} %gather_panel.1.source_blocks, bf16[512,128,128]{2,1,0:T(8,128)(2,1)} %tiles.3), custom_call_target="tpu_custom_call" | custom-call | tf_op jit(solution)/shard_map/apply_forward/pallas_call | solution.py:310
  35.0 30.5 %reduce_rows.1.source_blocks = bf16[112,64,128]{2,1,0:T(8,128)(2,1)} custom-call(bf16[112,64,128]{2,1,0:T(8,128)(2,1)} %apply_forward.1.part), custom_call_target="tpu_custom_call" | custom-call | tf_op jit(solution)/shard_map/reduce_rows/pallas_call | solution.py:446
  65.5 11.3 %apply_transposed.1 = (bf16[224,64,128]{2,1,0:T(8,128)(2,1)}, bf16[64,1792]{1,0:T(8,128)(2,1)}) custom-call(s32[512]{0:T(512)} %rows.3, s32[512]{0:T(512)} %cols.3, s32[1]{0:T(128)S(6)} %copy.7.count, bf16[112,64,128]{2,1,0:T(8,128)(2,1)} %reduce_rows.1.source_blocks, bf16[512,128,128]{2,1,0:T(8,128)(2,1)} %tiles.3), custom_call_target="tpu_custom_call" | custom-call | tf_op jit(solution)/shard_map/apply_transposed/pallas_call | solution.py:310
  76.8 31.9 %image_sums.1.sums = f32[64,1792]{1,0:T(8,128)} custom-call(bf16[224,64,128]{2,1,0:T(8,128)(2,1)} %get-tuple-element.5.part), custom_call_target="tpu_custom_call" | custom-call | tf_op jit(solution)/shard_map/image_sums/pallas_call | solution.py:556
  108.7 1.8 %leave.1 = f32[64,1792]{1,0:T(8,128)} custom-call(f32[64,1792]{1,0:T(8,128)} %image_sums.1.sums), custom_call_target="tpu_custom_call" | custom-call | tf_op jit(solution)/shard_map/leave/pallas_call | solution.py:574
